TPU v7x, 128 devices: a whole 4x4x4 slice. The times are simulated.
128 devices in a mesh: zone: 16 (over y, x), subzone: 8 (over z, core).
Axes of the slice: x: 4, y: 4, z: 4, core: 2. Of those that a mesh axis runs over, the one named last changes fastest.
Arguments:
- spectra: bfloat16 [32768, 2, 16, 512], P(('zone', 'subzone')), may hold values from -6 to 6
- pair_first: int32 [16384], P(('zone', 'subzone')), may hold values from 0 to 32767, as said below
- pair_second: int32 [16384], P(('zone', 'subzone')), may hold values from 0 to 32767, as said below
- pair_valid: int32 [16384], P(('zone', 'subzone')), may hold values 0 or 1
Outputs:
- pair_peak: float32 [16384], P(('zone', 'subzone'))
- coherence: float32 [32768], P(('zone', 'subzone'))
Inputs may be any that keep to these rules, and one draw needn't show every extreme that they name: `pair_first`: the pairs of block d (positions d * 128 onward, 128 of them) name as first sensor a sensor of block d (sensors d * 256 onward). `pair_second`: position q within block d names as second sensor a sensor of block (q), never the pair's first sensor.
All inputs are finite; a program needn't handle non-finite values. No bound on the sum of `pair_valid` on one device may be relied on, other than what follows from the above.
Results may differ from a plain program's by a relative error of at most 0.0028.
Values may be sent and summed in bfloat16 or wider, within the bound.
A program may use at most 128 MiB of HBM per device.

v0:
```python
import math

import jax
import jax.numpy as jnp
from jax import lax
from jax.sharding import PartitionSpec as P

LAGS = 512


def lag_table(bins, lags):
    bin_index = jnp.arange(bins, dtype=jnp.int32)[:, None]
    lag_index = jnp.arange(lags, dtype=jnp.int32)[None, :] - lags // 2
    phase = jnp.mod(bin_index * lag_index, 2 * bins).astype(jnp.float32) * (math.pi / bins)
    return jnp.concatenate([jnp.cos(phase), -jnp.sin(phase)], 0).astype(jnp.bfloat16)


def tile_peaks(first_spec, second_spec, table):
    first_re = first_spec[:, 0].astype(jnp.float32)
    first_im = first_spec[:, 1].astype(jnp.float32)
    second_re = second_spec[:, 0].astype(jnp.float32)
    second_im = second_spec[:, 1].astype(jnp.float32)
    cross_re = first_re * second_re + first_im * second_im
    cross_im = first_im * second_re - first_re * second_im
    divisor = jnp.maximum(jnp.sqrt(cross_re * cross_re + cross_im * cross_im), 1.0)
    whitened = jnp.concatenate([cross_re / divisor, cross_im / divisor], -1).astype(jnp.bfloat16)
    correlation = jnp.einsum("psk,kl->psl", whitened, table, preferred_element_type=jnp.float32)
    bins = first_spec.shape[-1]
    averaged = jnp.sum(correlation, axis=1) * (bins ** (-0.5) / first_spec.shape[2])
    return jnp.max(averaged, axis=-1)


def on_device(spectra, pair_first, pair_second, pair_valid):
    owners = lax.axis_size(("zone", "subzone"))
    sensors_here = spectra.shape[0]
    pair_count = pair_first.shape[0]
    slots = pair_count // owners
    trailing = spectra.shape[1:]
    offset = lax.axis_index(("zone", "subzone")) * sensors_here
    first_local = pair_first - offset
    wanted = (pair_second % sensors_here).reshape(owners, slots)
    asked_rows = lax.all_to_all(
        wanted, ("zone", "subzone"), split_axis=0, concat_axis=0, tiled=True
    )
    served = jnp.take(spectra, asked_rows.reshape(-1), axis=0).reshape((owners, slots) + trailing)
    partner = lax.all_to_all(served, ("zone", "subzone"), split_axis=0, concat_axis=0, tiled=True)
    partner = partner.reshape((pair_count,) + trailing)
    own_spec = jnp.take(spectra, first_local, axis=0)
    table = lag_table(spectra.shape[-1], LAGS)
    width = min(128, pair_count)
    tiles = pair_count // width

    def run_tile(items):
        return tile_peaks(items[0], items[1], table)

    peaks = lax.map(
        run_tile,
        (own_spec.reshape((tiles, width) + trailing), partner.reshape((tiles, width) + trailing)),
    ).reshape(-1)
    values = peaks * pair_valid.astype(jnp.float32)
    returned = lax.all_to_all(
        values.reshape(owners, slots), ("zone", "subzone"), split_axis=0, concat_axis=0, tiled=True
    )
    sensor_ids = jnp.arange(sensors_here, dtype=jnp.int32)[None, :]
    hits_first = (first_local[:, None] == sensor_ids).astype(jnp.float32)
    hits_second = (asked_rows.reshape(-1)[:, None] == sensor_ids).astype(jnp.float32)
    coherence = jnp.dot(values, hits_first, precision=lax.Precision.HIGHEST)
    coherence = coherence + jnp.dot(
        returned.reshape(-1), hits_second, precision=lax.Precision.HIGHEST
    )
    return (values, coherence)


def solution(mesh):
    return jax.shard_map(
        on_device,
        mesh=mesh,
        in_specs=(
            P(("zone", "subzone"), None, None, None),
            P(("zone", "subzone")),
            P(("zone", "subzone")),
            P(("zone", "subzone")),
        ),
        out_specs=(P(("zone", "subzone")), P(("zone", "subzone"))),
        check_vma=False,
    )
```

profile of v0, /device:TPU:1, one launch (start us, length us, event | category | flops | bytes accessed | tf_op | source)
XLA Modules:
  0.0 121.0 jit_solution(215019988759238948)
XLA Ops:
  0.6 0.7 fusion.23
  1.3 0.1 copy.19
  1.4 20.7 %all_to_all.23 = s32[128,1,1]{2,1,0:T(1,128)S(1)} all-to-all(s32[128,1,1]{2,1,0:T(1,128)S(1)} %copy.19), channel_id=1, replica_groups=mesh['zone'=16,'subzone'=8] {'zone','subzone'}, dimensions={0} | all-to-all | bytes 1024 | tf_op jit(solution)/shard_map/all_to_all | solution.py:42
  22.1 2.3 %reduce = s32[128]{0:T(128)S(1)} reduce(s32[128,1,1]{2,1,0:T(1,128)S(1)} %all_to_all.23, s32[]{:T(128)} %constant.68.clone.1), dimensions={1,2}, to_apply=%all_to_all.16.reduce_sub_computation | reduce | bytes 1028 | tf_op jit(solution)/shard_map/all_to_all | solution.py:42
  24.5 6.2 %gather_fusion.1 = bf16[128,2,16,512]{3,2,1,0:T(8,128)(2,1)} fusion(bf16[256,2,16,512]{3,2,1,0:T(8,128)(2,1)} %param.6, s32[1024]{0:T(1024)S(1)} %pad_clamp_fusion), kind=kCustom, calls=%fused_computation.1.clone | custom fusion | bytes 8389120 | tf_op jit(solution)/shard_map/jit(_take)/gather | solution.py:45
  30.7 4.6 %select_bitcast_fusion = bf16[128,1,2,16,512]{4,3,2,1,0:T(8,128)(2,1)} fusion(bf16[128,2,16,512]{3,2,1,0:T(8,128)(2,1)} %gather_fusion.1, pred[128]{0:T(512)(128)(4,1)S(1)} %compare_and_fusion), kind=kLoop, calls=%fused_computation.16 | loop fusion | flops 2097152 | bytes 8388736 | tf_op jit(solution)/shard_map/reshape | solution.py:45
  35.3 5.9 %all-to-all-start.1 = ((bf16[128,1,2,16,512]{4,3,2,1,0:T(8,128)(2,1)}), bf16[128,1,2,16,512]{4,3,2,1,0:T(8,128)(2,1)}, u32[]{:S(2)}, u32[]{:S(2)}) async-start(bf16[128,1,2,16,512]{4,3,2,1,0:T(8,128)(2,1)} %select_bitcast_fusion), calls=%async_computation.1 | async-start | bytes 8388608 | tf_op jit(solution)/shard_map/all_to_all | solution.py:46
  41.2 6.2 %gather_fusion = bf16[128,2,16,512]{3,2,1,0:T(8,128)(2,1)} fusion(bf16[256,2,16,512]{3,2,1,0:T(8,128)(2,1)} %param.6, s32[1024]{0:T(1024)S(1)} %pad_clamp_fusion.1), kind=kCustom, calls=%fused_computation.clone | custom fusion | bytes 8389120 | tf_op jit(solution)/shard_map/jit(_take)/gather | solution.py:48
  47.4 4.4 %cosine_convert_fusion = (bf16[512,512]{1,0:T(8,128)(2,1)S(1)}, bf16[512,512]{1,0:T(8,128)(2,1)S(1)}) fusion(s32[512]{0:T(512)S(1)} %iota_add_fusion), kind=kLoop, calls=%fused_computation.31 | loop fusion | flops 4456448 | bytes 1050624 | tf_op jit(solution)/shard_map/convert
  51.8 9.0 %copy_select_fusion = bf16[128,2,16,512]{3,0,2,1:T(8,128)(2,1)} fusion(bf16[128,2,16,512]{3,2,1,0:T(8,128)(2,1)} %gather_fusion, pred[128]{0:T(512)(128)(4,1)S(1)} %get-tuple-element.13), kind=kLoop, calls=%fused_computation.15 | loop fusion | flops 2097152 | bytes 8388736 | tf_op jit(solution)/shard_map/jit(_take)/select_n | solution.py:48
  60.8 33.1 %all-to-all-done.1 = bf16[128,1,2,16,512]{4,3,2,1,0:T(8,128)(2,1)} async-done(((bf16[128,1,2,16,512]{4,3,2,1,0:T(8,128)(2,1)}), bf16[128,1,2,16,512]{4,3,2,1,0:T(8,128)(2,1)}, u32[]{:S(2)}, u32[]{:S(2)}) %all-to-all-start.1) | async-done | bytes 4194336 | tf_op jit(solution)/shard_map/all_to_all | solution.py:46
  93.9 4.7 %copy.25 = bf16[128,1,2,16,512]{4,0,3,2,1:T(8,128)(2,1)S(1)} copy(bf16[128,1,2,16,512]{4,3,2,1,0:T(8,128)(2,1)} %all-to-all-done.1) | data formatting | bytes 8388608 | tf_op jit(solution)/shard_map/all_to_all | solution.py:46
  98.6 3.4 %divide_convert_fusion.1 = (bf16[128,16,512]{2,0,1:T(8,128)(2,1)S(1)}, bf16[128,16,512]{2,0,1:T(8,128)(2,1)S(1)}) fusion(bf16[128,2,16,512]{3,0,2,1:T(8,128)(2,1)S(1)} %bitcast.33, bf16[128,2,16,512]{3,0,2,1:T(8,128)(2,1)S(1)} %copy-done), kind=kLoop, calls=%fused_computation.18 | loop fusion | flops 18874368 | bytes 12582912 | tf_op jit(solution)/shard_map/convert.2
  102.0 0.0 copy-start.3
  102.0 2.3 %fusion.8 = f32[128,512]{1,0:T(8,128)S(1)} fusion(bf16[128,16,512]{2,0,1:T(8,128)(2,1)S(1)} %get-tuple-element.21, bf16[128,16,512]{2,0,1:T(8,128)(2,1)S(1)} %get-tuple-element.20, bf16[512,512]{1,0:T(8,128)(2,1)S(1)} %get-tuple-element.23, bf16[512,512]{1,0:T(8,128)(2,1)S(1)} %get-tuple-element.22), kind=kOutput, calls=%fused_computation.20 | convolution fusion | flops 2158952448 | bytes 5505024 | tf_op jit(solution)/shard_map/while/body/eval_jaxpr/psk,kl->psl/dot_general | solution.py:27
  104.3 0.1 multiply_reduce_fusion
  104.5 0.0 copy-start.1
  104.5 0.7 copy.22
  105.2 4.5 %all-to-all-start.2 = ((f32[128,1,1]{2,1,0:T(1,128)}), f32[128,1,1]{2,1,0:T(1,128)S(1)}, u32[]{:S(2)}, u32[]{:S(2)}) async-start(f32[128,1,1]{2,1,0:T(1,128)} %copy.22), calls=%async_computation.2 | async-start | bytes 131072 | tf_op jit(solution)/shard_map/all_to_all | solution.py:61
  109.7 0.2 fusion.19
  109.9 9.3 %all-to-all-done.2 = f32[128,1,1]{2,1,0:T(1,128)S(1)} async-done(((f32[128,1,1]{2,1,0:T(1,128)}), f32[128,1,1]{2,1,0:T(1,128)S(1)}, u32[]{:S(2)}, u32[]{:S(2)}) %all-to-all-start.2) | async-done | bytes 544 | tf_op jit(solution)/shard_map/all_to_all | solution.py:61
  119.2 1.0 reduce.1
  120.2 0.2 fusion.20
  120.4 0.6 add.51
  (14 shorter events, 0.1 us)
Async XLA Ops:
  35.3 5.9 %copy-start.2 = (s32[128]{0:T(128)S(1)}, s32[128]{0:T(128)}, u32[]{:S(2)}) copy-start(s32[128]{0:T(128)} %param.7) | copy-start | bytes 1540
  35.3 58.6 %all-to-all-start.1 = ((bf16[128,1,2,16,512]{4,3,2,1,0:T(8,128)(2,1)}), bf16[128,1,2,16,512]{4,3,2,1,0:T(8,128)(2,1)}, u32[]{:S(2)}, u32[]{:S(2)}) async-start(bf16[128,1,2,16,512]{4,3,2,1,0:T(8,128)(2,1)} %select_bitcast_fusion), calls=%async_computation.1 | async-start | bytes 8388608 | tf_op jit(solution)/shard_map/all_to_all | solution.py:46
  93.9 4.7 %copy-start = (bf16[128,2,16,512]{3,0,2,1:T(8,128)(2,1)S(1)}, bf16[128,2,16,512]{3,0,2,1:T(8,128)(2,1)}, u32[]{:S(2)}) copy-start(bf16[128,2,16,512]{3,0,2,1:T(8,128)(2,1)} %copy_select_fusion) | copy-start | bytes 12582916
  102.0 2.4 %copy-start.3 = (s32[128]{0:T(128)S(1)}, s32[128]{0:T(128)}, u32[]{:S(2)}) copy-start(s32[128]{0:T(128)} %param.9) | copy-start | bytes 1540
  104.5 16.6 %copy-start.1 = (f32[128]{0:T(128)}, f32[128]{0:T(128)S(1)}, u32[]{:S(2)}) copy-start(f32[128]{0:T(128)S(1)} %convert_multiply_fusion.4) | copy-start | bytes 1540
  105.2 14.0 %all-to-all-start.2 = ((f32[128,1,1]{2,1,0:T(1,128)}), f32[128,1,1]{2,1,0:T(1,128)S(1)}, u32[]{:S(2)}, u32[]{:S(2)}) async-start(f32[128,1,1]{2,1,0:T(1,128)} %copy.22), calls=%async_computation.2 | async-start | bytes 131072 | tf_op jit(solution)/shard_map/all_to_all | solution.py:61
where the time goes:
time: 121 us
  waiting for transfers between devices  42.3 us (35%)
  other arithmetic  26.3 us (22%)
  blocking collectives  20.7 us (17%)
  local copies, waits for them, and re-layouts  17.9 us (15%)
  starting transfers between devices  10.4 us (9%)
  matrix products  2.7 us (2%)
    all_to_all x1, waiting for transfers between devices, on_device(): lax.all_to_all(served, ('zone', 'subzone'), split_axis=0, concat_axis=0,...  33.1 us
    all_to_all x1, blocking collectives, on_device(): lax.all_to_all(wanted, ('zone', 'subzone'), split_axis=0, concat_axis=0,...  20.7 us
    all_to_all x1, waiting for transfers between devices, on_device(): lax.all_to_all(values.reshape(owners, slots), ('zone', 'subzone'), split_...  9.28 us
    select_n x2, other arithmetic, on_device(): own_spec = jnp.take(spectra, first_local, axis=0)  9.02 us
    another operation x2, other arithmetic  7.84 us
    gather x1, local copies, waits for them, and re-layouts, on_device(): own_spec = jnp.take(spectra, first_local, axis=0)  6.17 us
    gather x1, local copies, waits for them, and re-layouts, on_device(): jnp.take(spectra, asked_rows.reshape(-1), axis=0)  6.16 us
    all_to_all x1, starting transfers between devices, on_device(): lax.all_to_all(served, ('zone', 'subzone'), split_axis=0, concat_axis=0,...  5.86 us
  transfers between devices with their start and end apart: 2, of which 2 were waited for; matrix products, arithmetic and copies ran while one was open for 16% of the time, Pallas kernels for 0%

commit v1 on v0

v1 whole, which is shorter than its diff:
```python
import itertools
import math

import jax
import jax.numpy as jnp
import numpy as np
from jax import lax
from jax.experimental import pallas as pl
from jax.experimental.pallas import tpu as pltpu
from jax.sharding import PartitionSpec as P

LAGS = 512
MESH = pl.DeviceIdType.MESH
SIDES = (4, 4, 4, 2)
STRIDES = (32, 8, 2, 1)
GROUP = 8


def lag_table(bins, lags):
    phase = np.mod(np.arange(bins)[:, None] * (np.arange(lags)[None, :] - lags // 2), 2 * bins)
    phase = phase.astype(np.float64) * (math.pi / bins)
    table = np.concatenate([np.cos(phase), -np.sin(phase)], 0)
    return jnp.asarray(table.astype(np.float32), dtype=jnp.bfloat16)


def offsets():
    seen, orbits = set(), []
    for chip in itertools.product(range(4), repeat=3):
        orbit = []
        for turn in range(3):
            turned = chip[turn:] + chip[:turn]
            for way in (turned, tuple(-a % 4 for a in turned)):
                if way not in seen:
                    seen.add(way)
                    orbit.append(way)
        if orbit:
            orbits.append(orbit)
    hops = lambda orbit: sum(min(a, 4 - a) for a in orbit[0])
    orbits.sort(key=lambda orbit: -hops(orbit))
    order = [chip + (core,) for orbit in orbits for core in range(2) for chip in orbit]
    order.remove((0, 0, 0, 0))
    return [(0, 0, 0, 0)] + order


def place(block):
    return (block // 8, block % 8)


def kernel(
    spectra_hbm, first_ref, second_ref, valid_ref, table_hbm, peak_out, coherence_out,
    spectra, table, outgoing, arrived, whitened, codes_out, codes_in, codes, peaks, returned,
    own_rows, target, source,
    load_sem, send_sem, code_send_sem, peak_send_sem, recv_sem, code_sem, code_copy_sem, peak_sem,
):
    zone, subzone = lax.axis_index("zone"), lax.axis_index("subzone")
    me = zone * 8 + subzone
    sensors = spectra.shape[0]
    count = arrived.shape[0]
    groups = count // GROUP
    order = offsets()

    loads = [
        pltpu.make_async_copy(spectra_hbm, spectra, load_sem.at[0]),
        pltpu.make_async_copy(table_hbm, table, load_sem.at[1]),
    ]
    for load in loads:
        load.start()

    here = (zone // 4, zone % 4, subzone // 2, subzone % 2)
    ahead = [[(h + o) % n * s for o in range(n)] for h, n, s in zip(here, SIDES, STRIDES)]
    for k, offset in enumerate(order):
        target[k] = sum(ahead[a][o] for a, o in enumerate(offset))
        source[k] = sum(ahead[a][-o % SIDES[a]] for a, o in enumerate(offset))

    barrier = pltpu.get_barrier_semaphore()

    @pl.loop(1, count)
    def _(k):
        pl.semaphore_signal(barrier, inc=1, device_id=place(target[k]), device_id_type=MESH)

    @pl.loop(0, count)
    def _(k):
        pair = target[k]
        in_use = valid_ref[pair]
        row = pl.ds(k, 1)
        codes_out[row] = jnp.full((1, 128), second_ref[pair] % sensors + in_use * sensors, jnp.int32)
        own_rows[0, row] = jnp.full((1, 128), first_ref[pair] % sensors + (1 - in_use) * sensors, jnp.int32)
        own_rows[1, row] = jnp.full((1, 128), pair + (1 - in_use) * sensors, jnp.int32)

    pl.semaphore_wait(barrier, count - 1)

    def code_copy(k):
        return pltpu.make_async_remote_copy(
            src_ref=codes_out.at[pl.ds(k, 1)],
            dst_ref=codes_in.at[pl.ds(k, 1)],
            send_sem=code_send_sem,
            recv_sem=code_sem,
            device_id=place(target[k]),
            device_id_type=MESH,
        )

    def spectrum_copy(k):
        return pltpu.make_async_remote_copy(
            src_ref=outgoing.at[k],
            dst_ref=arrived.at[k],
            send_sem=send_sem,
            recv_sem=recv_sem.at[k // GROUP],
            device_id=place(target[k]),
            device_id_type=MESH,
        )

    def peak_copy(k):
        return pltpu.make_async_remote_copy(
            src_ref=peaks.at[pl.ds(k, 1)],
            dst_ref=returned.at[pl.ds(k, 1)],
            send_sem=peak_send_sem,
            recv_sem=peak_sem,
            device_id=place(source[k]),
            device_id_type=MESH,
        )

    @pl.loop(1, count)
    def _(k):
        code_copy(k).start()

    own_code = pltpu.make_async_copy(codes_out.at[pl.ds(0, 1)], codes_in.at[pl.ds(0, 1)], code_sem)
    own_code.start()
    loads[0].wait()
    outgoing[0] = spectra[first_ref[me] % sensors]
    own_spectrum = pltpu.make_async_copy(outgoing.at[0], arrived.at[0], recv_sem.at[0])
    own_spectrum.start()

    @pl.loop(1, count)
    def _(k):
        outgoing[k] = spectra[first_ref[target[k]] % sensors]
        spectrum_copy(k).start()

    pltpu.make_async_copy(codes_in, codes_in, code_sem).wait()
    copy = pltpu.make_async_copy(codes_in, codes, code_copy_sem)
    copy.start()
    copy.wait()
    loads[1].wait()

    segments, bins = spectra.shape[2:]
    depth = GROUP * segments
    row_of = lax.broadcasted_iota(jnp.int32, (GROUP, depth), 0)
    segment_of = lax.broadcasted_iota(jnp.int32, (GROUP, depth), 1)
    adder = jnp.where(segment_of // segments == row_of, 1.0, 0.0).astype(jnp.bfloat16)
    scale = bins ** (-0.5) / segments

    @pl.loop(0, groups)
    def _(g):
        here = pl.ds(g * GROUP, GROUP)
        pltpu.make_async_copy(arrived.at[here], arrived.at[here], recv_sem.at[g]).wait()
        for i in range(GROUP):
            k = g * GROUP + i
            b = codes[k, 0] % sensors
            first_re = arrived[k, 0].astype(jnp.float32)
            first_im = arrived[k, 1].astype(jnp.float32)
            second_re = spectra[b, 0].astype(jnp.float32)
            second_im = spectra[b, 1].astype(jnp.float32)
            cross_re = first_re * second_re + first_im * second_im
            cross_im = first_im * second_re - first_re * second_im
            factor = lax.rsqrt(jnp.maximum(cross_re * cross_re + cross_im * cross_im, 1.0))
            rows = pl.ds(i * segments, segments)
            whitened[rows, 0:bins] = (cross_re * factor).astype(jnp.bfloat16)
            whitened[rows, bins:] = (cross_im * factor).astype(jnp.bfloat16)
        summed = jnp.dot(adder, whitened[...], preferred_element_type=jnp.float32)
        high = summed.astype(jnp.bfloat16)
        low = (summed - high.astype(jnp.float32)).astype(jnp.bfloat16)
        both = jnp.dot(jnp.concatenate([high, low], 0), table[...], preferred_element_type=jnp.float32)
        correlation = (both[:GROUP] + both[GROUP:]) * scale
        peaks[here] = jnp.broadcast_to(jnp.max(correlation, axis=-1, keepdims=True), (GROUP, 128))

        @pl.loop(jnp.where(g == 0, 1, 0), GROUP)
        def _(i):
            peak_copy(g * GROUP + i).start()

    own_peak = pltpu.make_async_copy(peaks.at[pl.ds(0, 1)], returned.at[pl.ds(0, 1)], peak_sem)
    own_peak.start()

    lane = lax.broadcasted_iota(jnp.int32, (count, 128), 1)

    def pick(rows, first, values):
        return jnp.sum(jnp.where(rows == lane + first, values, 0.0), axis=0, keepdims=True)

    seconds = [pick(codes_in[...], sensors + first, peaks[...]) for first in range(0, sensors, 128)]
    pltpu.make_async_copy(returned, returned, peak_sem).wait()
    values = returned[...]
    for i, first in enumerate(range(0, sensors, 128)):
        coherence_out[:, pl.ds(first, 128)] = seconds[i] + pick(own_rows[0], first, values)
    peak_out[...] = pick(own_rows[1], 0, values)

    @pl.loop(1, count)
    def _(k):
        code_copy(k).wait_send()
        spectrum_copy(k).wait_send()
        peak_copy(k).wait_send()


def on_device(spectra, pair_first, pair_second, pair_valid):
    sensors, trailing = spectra.shape[0], spectra.shape[1:]
    count = pair_first.shape[0]
    segments, bins = trailing[1:]
    any_space, smem, vmem = pl.ANY, pltpu.SMEM, pltpu.VMEM
    peak, coherence = pl.pallas_call(
        kernel,
        out_shape=(
            jax.ShapeDtypeStruct((1, count), jnp.float32),
            jax.ShapeDtypeStruct((1, sensors), jnp.float32),
        ),
        in_specs=[
            pl.BlockSpec(memory_space=any_space),
            pl.BlockSpec(memory_space=smem),
            pl.BlockSpec(memory_space=smem),
            pl.BlockSpec(memory_space=smem),
            pl.BlockSpec(memory_space=any_space),
        ],
        out_specs=[pl.BlockSpec(memory_space=vmem)] * 2,
        scratch_shapes=[
            vmem((sensors,) + trailing, jnp.bfloat16),
            vmem((2 * bins, LAGS), jnp.bfloat16),
            vmem((count,) + trailing, jnp.bfloat16),
            vmem((count,) + trailing, jnp.bfloat16),
            vmem((GROUP * segments, 2 * bins), jnp.bfloat16),
            vmem((count, 128), jnp.int32),
            vmem((count, 128), jnp.int32),
            smem((count, 128), jnp.int32),
            vmem((count, 128), jnp.float32),
            vmem((count, 128), jnp.float32),
            vmem((2, count, 128), jnp.int32),
            smem((count,), jnp.int32),
            smem((count,), jnp.int32),
            pltpu.SemaphoreType.DMA((2,)),
            pltpu.SemaphoreType.DMA,
            pltpu.SemaphoreType.DMA,
            pltpu.SemaphoreType.DMA,
            pltpu.SemaphoreType.DMA((count // GROUP,)),
            pltpu.SemaphoreType.DMA,
            pltpu.SemaphoreType.DMA,
            pltpu.SemaphoreType.DMA,
        ],
        compiler_params=pltpu.CompilerParams(
            collective_id=1, has_side_effects=True, vmem_limit_bytes=40 << 20
        ),
    )(spectra, pair_first, pair_second, pair_valid, lag_table(bins, LAGS))
    return (peak.reshape(-1), coherence.reshape(-1))


def solution(mesh):
    blocks = ("zone", "subzone")
    return jax.shard_map(
        on_device,
        mesh=mesh,
        in_specs=(P(blocks, None, None, None), P(blocks), P(blocks), P(blocks)),
        out_specs=(P(blocks), P(blocks)),
        check_vma=False,
    )
```

time: 121 us -> 80.7 us (0.67)
  Pallas kernels: 0 us -> 72.2 us
  waiting for transfers between devices: 42.3 us -> 0 us
  other arithmetic: 26.3 us -> 0 us
  blocking collectives: 20.7 us -> 0 us
  starting transfers between devices: 10.4 us -> 0 us
  local copies, waits for them, and re-layouts: 17.9 us -> 7.64 us
  matrix products: 2.7 us -> 0 us
    pallas_call x0 -> x1, Pallas kernels: none -> 72.2 us  [on_device(): pl.pallas_call(kernel, out_shape=(jax.ShapeDtypeStruct((1, count), jnp.fl...]
    all_to_all x2 -> x0, waiting for transfers between devices: 42.3 us -> none  [the longest x1 33.1 us: on_device(): lax.all_to_all(served, ('zone', 'subzone'), split_axis=0, concat_axis=0,...]
    all_to_all x1 -> x0, blocking collectives: 20.7 us -> none  [on_device(): lax.all_to_all(wanted, ('zone', 'subzone'), split_axis=0, concat_axis=0,...]
    gather x2 -> x0, local copies, waits for them, and re-layouts: 12.3 us -> none  [the longest x1 6.17 us: on_device(): own_spec = jnp.take(spectra, first_local, axis=0)]
    all_to_all x2 -> x0, starting transfers between devices: 10.4 us -> none  [the longest x1 5.86 us: on_device(): lax.all_to_all(served, ('zone', 'subzone'), split_axis=0, concat_axis=0,...]
    select_n x3 -> x0, other arithmetic: 9.03 us -> none  [the longest x2 9.02 us: on_device(): own_spec = jnp.take(spectra, first_local, axis=0)]
    another operation x2 -> x0, other arithmetic: 7.84 us -> none
    unnamed x8 -> x12, local copies, waits for them, and re-layouts: 0.02 us -> 7.64 us
  transfers between devices with their start and end apart: 2 -> 0, of which waited for: 2 -> 0; matrix products, arithmetic and copies ran while one was open for 16% -> 0% of each run, Pallas kernels for 0% -> 0%
where the time goes in v1:
time: 80.7 us; the launch traced here: 80.5 us
  Pallas kernels  72.2 us (89%)
  local copies, waits for them, and re-layouts  7.64 us (9%)
    pallas_call x1, Pallas kernels, on_device(): pl.pallas_call(kernel, out_shape=(jax.ShapeDtypeStruct((1, count), jnp.fl...  72.2 us
    unnamed x12, local copies, waits for them, and re-layouts  7.64 us

profile of v1, /device:TPU:1, one launch (start us, length us, event | category | flops | bytes accessed | tf_op | source)
XLA Modules:
  0.0 80.5 jit_solution(16260498358869632757)
XLA Ops:
  0.6 0.0 copy-start
  0.6 3.4 %copy-done = bf16[256,2,16,512]{3,2,1,0:T(8,128)(2,1)S(1)} copy-done((bf16[256,2,16,512]{3,2,1,0:T(8,128)(2,1)S(1)}, bf16[256,2,16,512]{3,2,1,0:T(8,128)(2,1)}, u32[]{:S(2)}) %copy-start) | copy-done | bytes 8388632
  4.0 0.0 copy-start.1
  4.0 1.2 %copy-done.1 = bf16[1024,512]{1,0:T(8,128)(2,1)S(1)} copy-done((bf16[1024,512]{1,0:T(8,128)(2,1)S(1)}, bf16[1024,512]{1,0:T(8,128)(2,1)}, u32[]{:S(2)}) %copy-start.1) | copy-done | bytes 1048600
  5.2 0.0 copy-start.2
  5.2 0.7 copy-done.2
  5.9 0.0 copy-start.3
  5.9 0.7 copy-done.3
  6.5 0.0 copy-start.4
  6.6 0.7 copy-done.4
  7.2 72.2 %shard_map.68 = (f32[1,128]{1,0:T(1,128)S(1)}, f32[1,256]{1,0:T(1,128)S(1)}) custom-call(bf16[256,2,16,512]{3,2,1,0:T(8,128)(2,1)S(1)} %copy-done, s32[128]{0:T(128)S(1)} %copy-done.2, s32[128]{0:T(128)S(1)} %copy-done.3, s32[128]{0:T(128)S(1)} %copy-done.4, bf16[1024,512]{1,0:T(8,128)(2,1)S(1)} %copy-done.1), custom_call_target="tpu_custom_call" | custom-call | tf_op jit(solution)/shard_map/pallas_call | solution.py:206
  79.4 0.5 copy.9
  79.9 0.6 copy.10
Async XLA Ops:
  0.6 3.4 %copy-start = (bf16[256,2,16,512]{3,2,1,0:T(8,128)(2,1)S(1)}, bf16[256,2,16,512]{3,2,1,0:T(8,128)(2,1)}, u32[]{:S(2)}) copy-start(bf16[256,2,16,512]{3,2,1,0:T(8,128)(2,1)} %spectra_hbm.1) | copy-start | bytes 25165828
  4.0 1.2 %copy-start.1 = (bf16[1024,512]{1,0:T(8,128)(2,1)S(1)}, bf16[1024,512]{1,0:T(8,128)(2,1)}, u32[]{:S(2)}) copy-start(bf16[1024,512]{1,0:T(8,128)(2,1)} %constant.2.clone.table_hbm) | copy-start | bytes 3145732
  5.2 0.7 copy-start.2
  5.9 0.7 copy-start.3
  6.5 0.7 copy-start.4

commit v2 on v1

--- a/solution.py
+++ b/solution.py
@@ -23,23 +23,37 @@
     return jnp.asarray(table.astype(np.float32), dtype=jnp.bfloat16)
 
 
+def orbit(chip):
+    found = []
+    for turn in range(3):
+        turned = chip[turn:] + chip[:turn]
+        for way in (turned, tuple(-a % 4 for a in turned)):
+            if way not in found:
+                found.append(way)
+    return found
+
+
+IN_LINE = [((2, 0, 0), (0, 1))]
+IN_PLANE = [((2, 2, 0), (0, 1))]
+OTHERS = [
+    (chip, (0, 1))
+    for chip in (
+        (2, 2, 2), (1, 2, 2), (1, 1, 2), (1, 3, 2), (1, 1, 3), (1, 1, 1),
+        (1, 2, 0), (2, 1, 0), (1, 3, 0), (1, 1, 0), (1, 0, 0),
+    )
+]
+
+
+def spread(parts):
+    return [way + (core,) for chip, cores in parts for core in cores for way in orbit(chip)]
+
+
 def offsets():
-    seen, orbits = set(), []
-    for chip in itertools.product(range(4), repeat=3):
-        orbit = []
-        for turn in range(3):
-            turned = chip[turn:] + chip[:turn]
-            for way in (turned, tuple(-a % 4 for a in turned)):
-                if way not in seen:
-                    seen.add(way)
-                    orbit.append(way)
-        if orbit:
-            orbits.append(orbit)
-    hops = lambda orbit: sum(min(a, 4 - a) for a in orbit[0])
-    orbits.sort(key=lambda orbit: -hops(orbit))
-    order = [chip + (core,) for orbit in orbits for core in range(2) for chip in orbit]
-    order.remove((0, 0, 0, 0))
-    return [(0, 0, 0, 0)] + order
+    first = [(0, 0, 0, 0), (0, 0, 0, 1)] + spread(IN_LINE)
+    second = first + spread(IN_PLANE)
+    order = second + spread(OTHERS)
+    assert len(set(order)) == len(order) == 128
+    return order, len(first), len(second)
 
 
 def place(block):
@@ -47,36 +61,48 @@
 
 
 def kernel(
-    spectra_hbm, first_ref, second_ref, valid_ref, table_hbm, peak_out, coherence_out,
+    spectra_hbm, first_hbm, second_hbm, valid_hbm, table_hbm, peak_out, coherence_out,
     spectra, table, outgoing, arrived, whitened, codes_out, codes_in, codes, peaks, returned,
-    own_rows, target, source,
-    load_sem, send_sem, code_send_sem, peak_send_sem, recv_sem, code_sem, code_copy_sem, peak_sem,
+    own_rows, first_ref, second_ref, valid_ref, target, source,
+    load_sem, send_sem, code_send_sem, peak_send_sem, recv_sem, code_sem, code_copy_sem, peak_sem, plane_sem, cube_sem,
 ):
     zone, subzone = lax.axis_index("zone"), lax.axis_index("subzone")
     me = zone * 8 + subzone
     sensors = spectra.shape[0]
     count = arrived.shape[0]
     groups = count // GROUP
-    order = offsets()
+    order, lines, planes = offsets()
 
     loads = [
-        pltpu.make_async_copy(spectra_hbm, spectra, load_sem.at[0]),
-        pltpu.make_async_copy(table_hbm, table, load_sem.at[1]),
+        pltpu.make_async_copy(a, b, load_sem.at[i])
+        for i, (a, b) in enumerate(
+            [(first_hbm, first_ref), (second_hbm, second_ref), (valid_hbm, valid_ref), (spectra_hbm, spectra), (table_hbm, table)]
+        )
     ]
     for load in loads:
         load.start()
 
     here = (zone // 4, zone % 4, subzone // 2, subzone % 2)
     ahead = [[(h + o) % n * s for o in range(n)] for h, n, s in zip(here, SIDES, STRIDES)]
+
+    def signal(semaphore, ways):
+        for way in ways:
+            other = sum(ahead[a][o] for a, o in enumerate(way))
+            pl.semaphore_signal(semaphore, inc=1, device_id=place(other), device_id_type=MESH)
+
+    along_y = [(i, 0, 0, 0) for i in (1, 3, 2)]
+    along_x = [(0, i, 0, 0) for i in (1, 3, 2)]
+    barrier = pltpu.get_barrier_semaphore()
+    in_line = [
+        way[:3] + (core,) for i in (2, 1, 3) for way in ((i, 0, 0), (0, i, 0), (0, 0, i)) for core in range(2)
+    ] + [(0, 0, 0, 1)]
+    signal(barrier, in_line)
+
     for k, offset in enumerate(order):
         target[k] = sum(ahead[a][o] for a, o in enumerate(offset))
         source[k] = sum(ahead[a][-o % SIDES[a]] for a, o in enumerate(offset))
-
-    barrier = pltpu.get_barrier_semaphore()
-
-    @pl.loop(1, count)
-    def _(k):
-        pl.semaphore_signal(barrier, inc=1, device_id=place(target[k]), device_id_type=MESH)
+    for load in loads[:3]:
+        load.wait()
 
     @pl.loop(0, count)
     def _(k):
@@ -87,7 +113,7 @@
         own_rows[0, row] = jnp.full((1, 128), first_ref[pair] % sensors + (1 - in_use) * sensors, jnp.int32)
         own_rows[1, row] = jnp.full((1, 128), pair + (1 - in_use) * sensors, jnp.int32)
 
-    pl.semaphore_wait(barrier, count - 1)
+    loads[3].wait()
 
     def code_copy(k):
         return pltpu.make_async_remote_copy(
@@ -119,27 +145,36 @@
             device_id_type=MESH,
         )
 
+    def send(low, high):
+        @pl.loop(low, high)
+        def _(k):
+            outgoing[k] = spectra[first_ref[target[k]] % sensors]
+            spectrum_copy(k).start()
+
+    own_code = pltpu.make_async_copy(codes_out.at[pl.ds(0, 1)], codes_in.at[pl.ds(0, 1)], code_sem)
+    own_code.start()
+    outgoing[0] = spectra[first_ref[me] % sensors]
+    own_spectrum = pltpu.make_async_copy(outgoing.at[0], arrived.at[0], recv_sem.at[0])
+    own_spectrum.start()
+    pl.semaphore_wait(barrier, len(in_line))
+    signal(plane_sem, along_x + along_y)
+    send(1, lines)
+    pl.semaphore_wait(plane_sem, 6)
+    signal(cube_sem, along_x)
+    send(lines, planes)
+    pl.semaphore_wait(cube_sem, 3)
+
     @pl.loop(1, count)
     def _(k):
         code_copy(k).start()
 
-    own_code = pltpu.make_async_copy(codes_out.at[pl.ds(0, 1)], codes_in.at[pl.ds(0, 1)], code_sem)
-    own_code.start()
-    loads[0].wait()
-    outgoing[0] = spectra[first_ref[me] % sensors]
-    own_spectrum = pltpu.make_async_copy(outgoing.at[0], arrived.at[0], recv_sem.at[0])
-    own_spectrum.start()
-
-    @pl.loop(1, count)
-    def _(k):
-        outgoing[k] = spectra[first_ref[target[k]] % sensors]
-        spectrum_copy(k).start()
+    send(planes, count)
 
     pltpu.make_async_copy(codes_in, codes_in, code_sem).wait()
     copy = pltpu.make_async_copy(codes_in, codes, code_copy_sem)
     copy.start()
     copy.wait()
-    loads[1].wait()
+    loads[4].wait()
 
     segments, bins = spectra.shape[2:]
     depth = GROUP * segments
@@ -185,37 +220,28 @@
         return jnp.sum(jnp.where(rows == lane + first, values, 0.0), axis=0, keepdims=True)
 
     seconds = [pick(codes_in[...], sensors + first, peaks[...]) for first in range(0, sensors, 128)]
+    sent = pl.ds(1, count - 1)
+    for buffer, semaphore in ((codes_out, code_send_sem), (outgoing, send_sem), (peaks, peak_send_sem)):
+        pltpu.make_async_copy(buffer.at[sent], buffer.at[sent], semaphore).wait()
     pltpu.make_async_copy(returned, returned, peak_sem).wait()
     values = returned[...]
     for i, first in enumerate(range(0, sensors, 128)):
         coherence_out[:, pl.ds(first, 128)] = seconds[i] + pick(own_rows[0], first, values)
     peak_out[...] = pick(own_rows[1], 0, values)
 
-    @pl.loop(1, count)
-    def _(k):
-        code_copy(k).wait_send()
-        spectrum_copy(k).wait_send()
-        peak_copy(k).wait_send()
-
 
 def on_device(spectra, pair_first, pair_second, pair_valid):
     sensors, trailing = spectra.shape[0], spectra.shape[1:]
     count = pair_first.shape[0]
     segments, bins = trailing[1:]
-    any_space, smem, vmem = pl.ANY, pltpu.SMEM, pltpu.VMEM
+    hbm, smem, vmem = pltpu.HBM, pltpu.SMEM, pltpu.VMEM
     peak, coherence = pl.pallas_call(
         kernel,
         out_shape=(
             jax.ShapeDtypeStruct((1, count), jnp.float32),
             jax.ShapeDtypeStruct((1, sensors), jnp.float32),
         ),
-        in_specs=[
-            pl.BlockSpec(memory_space=any_space),
-            pl.BlockSpec(memory_space=smem),
-            pl.BlockSpec(memory_space=smem),
-            pl.BlockSpec(memory_space=smem),
-            pl.BlockSpec(memory_space=any_space),
-        ],
+        in_specs=[pl.BlockSpec(memory_space=hbm)] * 5,
         out_specs=[pl.BlockSpec(memory_space=vmem)] * 2,
         scratch_shapes=[
             vmem((sensors,) + trailing, jnp.bfloat16),
@@ -231,7 +257,10 @@
             vmem((2, count, 128), jnp.int32),
             smem((count,), jnp.int32),
             smem((count,), jnp.int32),
-            pltpu.SemaphoreType.DMA((2,)),
+            smem((count,), jnp.int32),
+            smem((count,), jnp.int32),
+            smem((count,), jnp.int32),
+            pltpu.SemaphoreType.DMA((5,)),
             pltpu.SemaphoreType.DMA,
             pltpu.SemaphoreType.DMA,
             pltpu.SemaphoreType.DMA,
@@ -239,9 +268,11 @@
             pltpu.SemaphoreType.DMA,
             pltpu.SemaphoreType.DMA,
             pltpu.SemaphoreType.DMA,
+            pltpu.SemaphoreType.REGULAR,
+            pltpu.SemaphoreType.REGULAR,
         ],
         compiler_params=pltpu.CompilerParams(
-            collective_id=1, has_side_effects=True, vmem_limit_bytes=40 << 20
+            collective_id=1, has_side_effects=True, vmem_limit_bytes=60 << 20
         ),
     )(spectra, pair_first, pair_second, pair_valid, lag_table(bins, LAGS))
     return (peak.reshape(-1), coherence.reshape(-1))

time: 80.7 us -> 69.4 us (0.86)
  Pallas kernels: 72.2 us -> 66.2 us
  local copies, waits for them, and re-layouts: 7.64 us -> 2.36 us
    pallas_call x1, Pallas kernels: 72.2 us -> 66.2 us  [on_device(): pl.pallas_call(kernel, out_shape=(jax.ShapeDtypeStruct((1, count), jnp.fl...]
    unnamed x12 -> x2, local copies, waits for them, and re-layouts: 7.64 us -> 2.36 us
where the time goes in v2:
time: 69.4 us; the launch traced here: 69.2 us
  Pallas kernels  66.2 us (95%)
  local copies, waits for them, and re-layouts  2.36 us (3%)
    pallas_call x1, Pallas kernels, on_device(): pl.pallas_call(kernel, out_shape=(jax.ShapeDtypeStruct((1, count), jnp.fl...  66.2 us
    unnamed x2, local copies, waits for them, and re-layouts  2.36 us

profile of v2, /device:TPU:1, one launch (start us, length us, event | category | flops | bytes accessed | tf_op | source)
XLA Modules:
  0.0 69.2 jit_solution(4246808701823916278)
XLA Ops:
  0.6 66.2 %shard_map.68 = (f32[1,128]{1,0:T(1,128)}, f32[1,256]{1,0:T(1,128)}) custom-call(bf16[256,2,16,512]{3,2,1,0:T(8,128)(2,1)} %spectra_hbm.1, s32[128]{0:T(128)} %first_hbm.1, s32[128]{0:T(128)} %second_hbm.1, s32[128]{0:T(128)} %valid_hbm.1, bf16[1024,512]{1,0:T(8,128)(2,1)} %constant.2.clone.table_hbm), custom_call_target="tpu_custom_call" | custom-call | tf_op jit(solution)/shard_map/pallas_call | solution.py:238
  66.9 1.1 %copy.9 = f32[128]{0:T(128)} copy(f32[128]{0:T(128)} %bitcast.3) | data formatting | bytes 1024
  68.0 1.2 %copy.10 = f32[256]{0:T(256)} copy(f32[256]{0:T(256)} %bitcast.2) | data formatting | bytes 2048

commit v3 on v2

--- a/solution.py
+++ b/solution.py
@@ -14,6 +14,7 @@
 SIDES = (4, 4, 4, 2)
 STRIDES = (32, 8, 2, 1)
 GROUP = 8
+CODES_AT = 16
 
 
 def lag_table(bins, lags):
@@ -62,7 +63,7 @@
 
 def kernel(
     spectra_hbm, first_hbm, second_hbm, valid_hbm, table_hbm, peak_out, coherence_out,
-    spectra, table, outgoing, arrived, whitened, codes_out, codes_in, codes, peaks, returned,
+    spectra, table, outgoing, arrived, whitened, codes_out, codes_in, code_row, codes, peaks, returned,
     own_rows, first_ref, second_ref, valid_ref, target, source,
     load_sem, send_sem, code_send_sem, peak_send_sem, recv_sem, code_sem, code_copy_sem, peak_sem, plane_sem, cube_sem,
 ):
@@ -76,10 +77,15 @@
     loads = [
         pltpu.make_async_copy(a, b, load_sem.at[i])
         for i, (a, b) in enumerate(
-            [(first_hbm, first_ref), (second_hbm, second_ref), (valid_hbm, valid_ref), (spectra_hbm, spectra), (table_hbm, table)]
+            [(first_hbm, first_ref), (second_hbm, second_ref), (valid_hbm, valid_ref), (table_hbm, table)]
         )
     ]
-    for load in loads:
+    share = sensors // 4
+    parts = tuple(
+        pltpu.make_async_copy(spectra_hbm.at[pl.ds(i * share, share)], spectra.at[pl.ds(i * share, share)], load_sem.at[4 + i])
+        for i in range(4)
+    )
+    for load in (loads[0],) + parts + tuple(loads[1:]):
         load.start()
 
     here = (zone // 4, zone % 4, subzone // 2, subzone % 2)
@@ -98,22 +104,15 @@
     ] + [(0, 0, 0, 1)]
     signal(barrier, in_line)
 
-    for k, offset in enumerate(order):
-        target[k] = sum(ahead[a][o] for a, o in enumerate(offset))
-        source[k] = sum(ahead[a][-o % SIDES[a]] for a, o in enumerate(offset))
-    for load in loads[:3]:
+    def locate(low, high):
+        for k in range(low, high):
+            target[k] = sum(ahead[a][o] for a, o in enumerate(order[k]))
+
+    pl.semaphore_wait(barrier, len(in_line))
+    signal(plane_sem, along_x + along_y)
+    locate(0, planes)
+    for load in (loads[0],) + parts:
         load.wait()
-
-    @pl.loop(0, count)
-    def _(k):
-        pair = target[k]
-        in_use = valid_ref[pair]
-        row = pl.ds(k, 1)
-        codes_out[row] = jnp.full((1, 128), second_ref[pair] % sensors + in_use * sensors, jnp.int32)
-        own_rows[0, row] = jnp.full((1, 128), first_ref[pair] % sensors + (1 - in_use) * sensors, jnp.int32)
-        own_rows[1, row] = jnp.full((1, 128), pair + (1 - in_use) * sensors, jnp.int32)
-
-    loads[3].wait()
 
     def code_copy(k):
         return pltpu.make_async_remote_copy(
@@ -145,36 +144,55 @@
             device_id_type=MESH,
         )
 
+    def pack(k):
+        outgoing[k] = spectra[first_ref[target[k]] % sensors]
+
     def send(low, high):
         @pl.loop(low, high)
         def _(k):
-            outgoing[k] = spectra[first_ref[target[k]] % sensors]
+            pack(k)
             spectrum_copy(k).start()
 
-    own_code = pltpu.make_async_copy(codes_out.at[pl.ds(0, 1)], codes_in.at[pl.ds(0, 1)], code_sem)
-    own_code.start()
-    outgoing[0] = spectra[first_ref[me] % sensors]
-    own_spectrum = pltpu.make_async_copy(outgoing.at[0], arrived.at[0], recv_sem.at[0])
-    own_spectrum.start()
-    pl.semaphore_wait(barrier, len(in_line))
-    signal(plane_sem, along_x + along_y)
     send(1, lines)
     pl.semaphore_wait(plane_sem, 6)
     signal(cube_sem, along_x)
     send(lines, planes)
+    locate(planes, count)
     pl.semaphore_wait(cube_sem, 3)
-
-    @pl.loop(1, count)
+    send(planes, CODES_AT)
+    for load in loads[1:3]:
+        load.wait()
+    for k, offset in enumerate(order):
+        source[k] = sum(ahead[a][-o % SIDES[a]] for a, o in enumerate(offset))
+
+    @pl.loop(0, count)
     def _(k):
-        code_copy(k).start()
-
-    send(planes, count)
+        pair = target[k]
+        in_use = valid_ref[pair]
+        row = pl.ds(k, 1)
+        codes_out[row] = jnp.full((1, 128), second_ref[pair] % sensors + in_use * sensors, jnp.int32)
+        own_rows[0, row] = jnp.full((1, 128), first_ref[pair] % sensors + (1 - in_use) * sensors, jnp.int32)
+        own_rows[1, row] = jnp.full((1, 128), pair + (1 - in_use) * sensors, jnp.int32)
+
+        @pl.when(k > 0)
+        def _():
+            code_copy(k).start()
+
+    pack(0)
+    own_spectrum = pltpu.make_async_copy(outgoing.at[0], arrived.at[0], recv_sem.at[0])
+    own_spectrum.start()
+    own_code = pltpu.make_async_copy(codes_out.at[pl.ds(0, 1)], codes_in.at[pl.ds(0, 1)], code_sem)
+    own_code.start()
+    send(CODES_AT, count)
 
     pltpu.make_async_copy(codes_in, codes_in, code_sem).wait()
-    copy = pltpu.make_async_copy(codes_in, codes, code_copy_sem)
+    lane = lax.broadcasted_iota(jnp.int32, (count, 128), 1)
+    slot = lax.broadcasted_iota(jnp.int32, (count, 128), 0)
+    code_row[...] = jnp.sum(jnp.where(lane == slot, codes_in[...], 0), axis=0, keepdims=True)
+    copy = pltpu.make_async_copy(code_row, codes, code_copy_sem)
     copy.start()
     copy.wait()
-    loads[4].wait()
+    loads[3].wait()
 
     segments, bins = spectra.shape[2:]
     depth = GROUP * segments
@@ -189,7 +207,7 @@
         pltpu.make_async_copy(arrived.at[here], arrived.at[here], recv_sem.at[g]).wait()
         for i in range(GROUP):
             k = g * GROUP + i
-            b = codes[k, 0] % sensors
+            b = codes[0, k] % sensors
             first_re = arrived[k, 0].astype(jnp.float32)
             first_im = arrived[k, 1].astype(jnp.float32)
             second_re = spectra[b, 0].astype(jnp.float32)
@@ -214,8 +232,6 @@
     own_peak = pltpu.make_async_copy(peaks.at[pl.ds(0, 1)], returned.at[pl.ds(0, 1)], peak_sem)
     own_peak.start()
 
-    lane = lax.broadcasted_iota(jnp.int32, (count, 128), 1)
-
     def pick(rows, first, values):
         return jnp.sum(jnp.where(rows == lane + first, values, 0.0), axis=0, keepdims=True)
 
@@ -238,8 +254,8 @@
     peak, coherence = pl.pallas_call(
         kernel,
         out_shape=(
-            jax.ShapeDtypeStruct((1, count), jnp.float32),
-            jax.ShapeDtypeStruct((1, sensors), jnp.float32),
+            vmem((1, count), jnp.float32),
+            vmem((1, sensors), jnp.float32),
         ),
         in_specs=[pl.BlockSpec(memory_space=hbm)] * 5,
         out_specs=[pl.BlockSpec(memory_space=vmem)] * 2,
@@ -251,7 +267,8 @@
             vmem((GROUP * segments, 2 * bins), jnp.bfloat16),
             vmem((count, 128), jnp.int32),
             vmem((count, 128), jnp.int32),
-            smem((count, 128), jnp.int32),
+            vmem((1, count), jnp.int32),
+            smem((1, count), jnp.int32),
             vmem((count, 128), jnp.float32),
             vmem((count, 128), jnp.float32),
             vmem((2, count, 128), jnp.int32),
@@ -260,7 +277,7 @@
             smem((count,), jnp.int32),
             smem((count,), jnp.int32),
             smem((count,), jnp.int32),
-            pltpu.SemaphoreType.DMA((5,)),
+            pltpu.SemaphoreType.DMA((8,)),
             pltpu.SemaphoreType.DMA,
             pltpu.SemaphoreType.DMA,
             pltpu.SemaphoreType.DMA,

time: 69.4 us -> 65.7 us (0.947)
  Pallas kernels: 66.2 us -> 63.9 us
  local copies, waits for them, and re-layouts: 2.36 us -> 1.08 us
    pallas_call x1, Pallas kernels: 66.2 us -> 63.9 us  [on_device(): pl.pallas_call(kernel, out_shape=(vmem((1, count), jnp.float32), vmem((1,...]
    unnamed x2, local copies, waits for them, and re-layouts: 2.36 us -> 1.08 us
where the time goes in v3:
time: 65.7 us; the launch traced here: 65.6 us
  Pallas kernels  63.9 us (97%)
  local copies, waits for them, and re-layouts  1.08 us (2%)
    pallas_call x1, Pallas kernels, on_device(): pl.pallas_call(kernel, out_shape=(vmem((1, count), jnp.float32), vmem((1,...  63.9 us

profile of v3, /device:TPU:1, one launch (start us, length us, event | category | flops | bytes accessed | tf_op | source)
XLA Modules:
  0.0 65.6 jit_solution(351413106556752150)
XLA Ops:
  0.6 63.9 %shard_map.68 = (f32[1,128]{1,0:T(1,128)S(1)}, f32[1,256]{1,0:T(1,128)S(1)}) custom-call(bf16[256,2,16,512]{3,2,1,0:T(8,128)(2,1)} %spectra_hbm.1, s32[128]{0:T(128)} %first_hbm.1, s32[128]{0:T(128)} %second_hbm.1, s32[128]{0:T(128)} %valid_hbm.1, bf16[1024,512]{1,0:T(8,128)(2,1)} %constant.2.clone.table_hbm), custom_call_target="tpu_custom_call" | custom-call | tf_op jit(solution)/shard_map/pallas_call | solution.py:254
  64.5 0.5 copy.9
  65.0 0.6 copy.10

commit v4 on v3

--- a/solution.py
+++ b/solution.py
@@ -46,7 +46,9 @@
 
 
 def spread(parts):
-    return [way + (core,) for chip, cores in parts for core in cores for way in orbit(chip)]
+    return [
+        way + ((i + core) % 2,) for chip, cores in parts for core in cores for i, way in enumerate(orbit(chip))
+    ]
 
 
 def offsets():

time: 65.7 us -> 65.2 us (level)
  no operation moved by 1% of the time
where the time goes in v4:
time: 65.2 us; the launch traced here: 65.1 us
  Pallas kernels  63.3 us (97%)
  local copies, waits for them, and re-layouts  1.08 us (2%)
    pallas_call x1, Pallas kernels, on_device(): pl.pallas_call(kernel, out_shape=(vmem((1, count), jnp.float32), vmem((1,...  63.3 us

profile of v4, /device:TPU:1, one launch (start us, length us, event | category | flops | bytes accessed | tf_op | source)
XLA Modules:
  0.0 65.1 jit_solution(6508218598675346213)
XLA Ops:
  0.6 63.3 %shard_map.68 = (f32[1,128]{1,0:T(1,128)S(1)}, f32[1,256]{1,0:T(1,128)S(1)}) custom-call(bf16[256,2,16,512]{3,2,1,0:T(8,128)(2,1)} %spectra_hbm.1, s32[128]{0:T(128)} %first_hbm.1, s32[128]{0:T(128)} %second_hbm.1, s32[128]{0:T(128)} %valid_hbm.1, bf16[1024,512]{1,0:T(8,128)(2,1)} %constant.2.clone.table_hbm), custom_call_target="tpu_custom_call" | custom-call | tf_op jit(solution)/shard_map/pallas_call | solution.py:256
  64.0 0.5 copy.9
  64.5 0.6 copy.10

commit v5 on v4

--- a/solution.py
+++ b/solution.py
@@ -173,8 +173,6 @@
         in_use = valid_ref[pair]
         row = pl.ds(k, 1)
         codes_out[row] = jnp.full((1, 128), second_ref[pair] % sensors + in_use * sensors, jnp.int32)
-        own_rows[0, row] = jnp.full((1, 128), first_ref[pair] % sensors + (1 - in_use) * sensors, jnp.int32)
-        own_rows[1, row] = jnp.full((1, 128), pair + (1 - in_use) * sensors, jnp.int32)
 
         @pl.when(k > 0)
         def _():
@@ -186,6 +184,14 @@
     own_code = pltpu.make_async_copy(codes_out.at[pl.ds(0, 1)], codes_in.at[pl.ds(0, 1)], code_sem)
     own_code.start()
     send(CODES_AT, count)
+
+    @pl.loop(0, count)
+    def _(k):
+        pair = target[k]
+        in_use = valid_ref[pair]
+        row = pl.ds(k, 1)
+        own_rows[0, row] = jnp.full((1, 128), first_ref[pair] % sensors + (1 - in_use) * sensors, jnp.int32)
+        own_rows[1, row] = jnp.full((1, 128), pair + (1 - in_use) * sensors, jnp.int32)
 
     pltpu.make_async_copy(codes_in, codes_in, code_sem).wait()
     lane = lax.broadcasted_iota(jnp.int32, (count, 128), 1)

time: 65.2 us -> 64.9 us (level)
  no operation moved by 1% of the time
where the time goes in v5:
time: 64.9 us; the launch traced here: 64.8 us
  Pallas kernels  63.1 us (97%)
  local copies, waits for them, and re-layouts  1.08 us (2%)
    pallas_call x1, Pallas kernels, on_device(): pl.pallas_call(kernel, out_shape=(vmem((1, count), jnp.float32), vmem((1,...  63.1 us

profile of v5, /device:TPU:1, one launch (start us, length us, event | category | flops | bytes accessed | tf_op | source)
XLA Modules:
  0.0 64.8 jit_solution(989172870251774455)
XLA Ops:
  0.6 63.1 %shard_map.68 = (f32[1,128]{1,0:T(1,128)S(1)}, f32[1,256]{1,0:T(1,128)S(1)}) custom-call(bf16[256,2,16,512]{3,2,1,0:T(8,128)(2,1)} %spectra_hbm.1, s32[128]{0:T(128)} %first_hbm.1, s32[128]{0:T(128)} %second_hbm.1, s32[128]{0:T(128)} %valid_hbm.1, bf16[1024,512]{1,0:T(8,128)(2,1)} %constant.2.clone.table_hbm), custom_call_target="tpu_custom_call" | custom-call | tf_op jit(solution)/shard_map/pallas_call | solution.py:262
  63.7 0.5 copy.9
  64.2 0.6 copy.10

commit v6 on v5

--- a/solution.py
+++ b/solution.py
@@ -39,7 +39,7 @@
 OTHERS = [
     (chip, (0, 1))
     for chip in (
-        (2, 2, 2), (1, 2, 2), (1, 1, 2), (1, 3, 2), (1, 1, 3), (1, 1, 1),
+        (1, 1, 1), (1, 1, 3), (1, 3, 2), (1, 1, 2), (1, 2, 2), (2, 2, 2),
         (1, 2, 0), (2, 1, 0), (1, 3, 0), (1, 1, 0), (1, 0, 0),
     )
 ]

time: 64.9 us -> 64.8 us (level)
  no operation moved by 1% of the time
where the time goes in v6:
time: 64.8 us; the launch traced here: 64.7 us
  Pallas kernels  63 us (97%)
  local copies, waits for them, and re-layouts  1.08 us (2%)
    pallas_call x1, Pallas kernels, on_device(): pl.pallas_call(kernel, out_shape=(vmem((1, count), jnp.float32), vmem((1,...  63 us

profile of v6, /device:TPU:1, one launch (start us, length us, event | category | flops | bytes accessed | tf_op | source)
XLA Modules:
  0.0 64.7 jit_solution(10989681402097818967)
XLA Ops:
  0.6 63.0 %shard_map.68 = (f32[1,128]{1,0:T(1,128)S(1)}, f32[1,256]{1,0:T(1,128)S(1)}) custom-call(bf16[256,2,16,512]{3,2,1,0:T(8,128)(2,1)} %spectra_hbm.1, s32[128]{0:T(128)} %first_hbm.1, s32[128]{0:T(128)} %second_hbm.1, s32[128]{0:T(128)} %valid_hbm.1, bf16[1024,512]{1,0:T(8,128)(2,1)} %constant.2.clone.table_hbm), custom_call_target="tpu_custom_call" | custom-call | tf_op jit(solution)/shard_map/pallas_call | solution.py:262
  63.7 0.5 copy.9
  64.2 0.6 copy.10
